TPU v7x, 1024 devices: a whole 8x8x8 slice. The times are simulated.
1024 devices in a mesh: dp: 64 (over x, y_lo, core), mp: 16 (over z, y_hi).
Axes of the slice: x: 8, y: 8 (y_hi: 2, y_lo: 4; y = y_hi * 4 + y_lo), z: 8, core: 2. Of those that a mesh axis runs over, the one named last changes fastest.
Arguments:
- activations: bfloat16 [16384, 8192], P('dp', 'mp'), may hold values from -6 to 6
- out_grads: bfloat16 [16384, 14336], P('dp', 'mp'), may hold values from -0.046875 to 0.046875
- basis: bfloat16 [8192, 1024], P('mp'), may hold values from -0.0625 to 0.0625
- first_moment: float32 [1024, 14336], P('dp', 'mp'), may hold values from -3 to 3
- second_moment: float32 [1024, 14336], P('dp', 'mp'), may hold values from 0.05 to 2
Outputs:
- weight_step: float32 [8192, 14336], P('dp', 'mp')
- new_first: float32 [1024, 14336], P('dp', 'mp')
- new_second: float32 [1024, 14336], P('dp', 'mp')
All inputs are finite; a program needn't handle non-finite values.
Results may differ from a plain program's by a relative error of at most 0.0031.
Values may be sent and summed in bfloat16 or wider, within the bound.
A program may use at most 32 MiB of HBM per device.

v0:
```python
import jax
import jax.numpy as jnp
from jax import lax
from jax.sharding import PartitionSpec as P

STEP = 10


beta_first = 0.9
beta_second = 0.95
adam_eps = 1e-08
galore_scale = 0.25


def spread(block, axis, owner):
    block = jnp.where(lax.axis_index(axis) == owner, block, jnp.zeros_like(block))
    return lax.psum(block, axis)


def body(activations, out_grads, basis, first_moment, second_moment):
    partial_value = jnp.dot(activations, basis, preferred_element_type=jnp.float32)
    summed = lax.psum(partial_value, "mp")
    projected = summed.astype(jnp.bfloat16)
    columns = projected
    gradient = lax.psum_scatter(
        lax.dot_general(
            columns, out_grads, (((0,), (0,)), ((), ())), preferred_element_type=jnp.float32
        ),
        "dp",
        scatter_dimension=0,
        tiled=True,
    )
    new_first = beta_first * first_moment + (1.0 - beta_first) * gradient
    new_second = beta_second * second_moment + (1.0 - beta_second) * gradient * gradient
    first_hat = new_first / (1.0 - beta_first**STEP)
    second_hat = new_second / (1.0 - beta_second**STEP)
    direction = (first_hat / (jnp.sqrt(second_hat) + adam_eps)).astype(jnp.bfloat16)
    block_ratio = lax.axis_size("dp") // lax.axis_size("mp")
    row_count = basis.shape[0] // block_ratio
    dp_place = lax.axis_index("dp")
    own_rows = lax.dynamic_slice_in_dim(basis, dp_place % block_ratio * row_count, row_count, 0)
    rows_here = spread(own_rows, "mp", dp_place // block_ratio)
    columns = rows_here
    update = jnp.dot(
        columns,
        lax.all_gather(direction, "dp", axis=0, tiled=True),
        preferred_element_type=jnp.float32,
    )
    return (galore_scale * update, new_first, new_second)


def solution(mesh):
    return jax.shard_map(
        body,
        mesh=mesh,
        in_specs=(P("dp", "mp"), P("dp", "mp"), P("mp", None), P("dp", "mp"), P("dp", "mp")),
        out_specs=(P("dp", "mp"), P("dp", "mp"), P("dp", "mp")),
        check_vma=False,
    )
```

profile of v0, /device:TPU:1, one launch (start us, length us, event | category | flops | bytes accessed | tf_op | source)
XLA Modules:
  0.0 607.5 jit_solution(5961501550788856987)
XLA Ops:
  8.0 0.0 copy-start
  8.0 0.0 reduce-scatter.2.cloned.1.call-start
  8.1 1.8 fusion.4
  9.8 138.5 %all-reduce.4 = bf16[256,1024]{1,0:T(8,128)(2,1)S(1)} all-reduce(f32[256,1024]{1,0:T(8,128)S(1)} %fusion.4), channel_id=1, replica_groups=mesh['dp'=64,'mp'=16] {'mp'}, use_global_device_ids=true, to_apply=%region_1.0 | all-reduce | flops 262144 | bytes 1572864 | tf_op jit(solution)/shard_map/psum | solution.py:22
  148.3 0.0 copy-done
  148.4 2.5 fusion.5
  150.9 0.0 copy-start.1
  150.9 0.0 copy-start.2
  150.9 0.0 reduce-scatter.2.cloned.1.call-update
  150.9 0.0 all-reduce.3.cloned.1.call-start
  151.0 1.7 dynamic-slice_select_fusion
  152.7 0.0 all-reduce.3.cloned.1.call-update
  152.7 0.0 all-gather.2.cloned.1.call-start
  152.8 321.1 %reduce-scatter.2.cloned.1.call-done = f32[16,896]{1,0:T(8,128)} async-done(((f32[1024,896]{1,0:T(8,128)}), f32[16,896]{1,0:T(8,128)}) %reduce-scatter.2.cloned.1.call-update) | async-done | bytes 57360 | tf_op jit(solution)/shard_map/reduce_scatter | solution.py:25
  473.9 0.0 copy-done.1
  473.9 0.0 copy-done.2
  473.9 1.5 divide_convert_fusion
  475.4 0.0 all-gather.2.cloned.1.call-update
  475.4 0.0 all-reduce.3.cloned.1.call-done
  475.5 121.8 %all-gather.2.cloned.1.call-done = bf16[1024,896]{1,0:T(8,128)(2,1)} async-done(((bf16[16,896]{1,0:T(8,128)(2,1)}), bf16[1024,896]{1,0:T(8,128)(2,1)}) %all-gather.2.cloned.1.call-update) | async-done | bytes 1835024 | tf_op jit(solution)/shard_map/all_gather | solution.py:46
  597.3 2.8 convolution_multiply_fusion
Async XLA Ops:
  8.0 140.4 %copy-start = (bf16[256,896]{1,0:T(8,128)(2,1)S(1)}, bf16[256,896]{1,0:T(8,128)(2,1)}, u32[]{:S(2)}) copy-start(bf16[256,896]{1,0:T(8,128)(2,1)} %param.6) | copy-start | bytes 1376260
  8.0 465.9 %reduce-scatter.2.cloned.1.call-start = ((), (), s32[]{:S(2)}) async-start(), calls=%async_computation.2 | async-start | bytes 3727360 | tf_op jit(solution)/shard_map/reduce_scatter | solution.py:25
  150.9 323.0 %copy-start.1 = (f32[16,896]{1,0:T(8,128)S(1)}, f32[16,896]{1,0:T(8,128)}, u32[]{:S(2)}) copy-start(f32[16,896]{1,0:T(8,128)} %param.8) | copy-start | bytes 172036
  150.9 323.0 %copy-start.2 = (f32[16,896]{1,0:T(8,128)S(1)}, f32[16,896]{1,0:T(8,128)}, u32[]{:S(2)}) copy-start(f32[16,896]{1,0:T(8,128)} %param.9) | copy-start | bytes 172036
  150.9 324.5 %all-reduce.3.cloned.1.call-start = ((), (), s32[]{:S(2)}) async-start(), calls=%async_computation.1 | async-start | bytes 524288 | tf_op jit(solution)/shard_map/psum | solution.py:17
  152.7 444.5 %all-gather.2.cloned.1.call-start = ((), (), s32[]{:S(2)}) async-start(), calls=%async_computation.3 | async-start | bytes 1863680 | tf_op jit(solution)/shard_map/all_gather | solution.py:46
Sparse Core Ops, SparseCore 0:
  151.0 322.8 reduce-scatter.1
  476.6 120.5 all-gather.1
Sparse Core Ops, SparseCore 1:
  155.4 228.7 all-reduce.2
where the time goes:
time: 608 us
  waiting for transfers between devices  443 us (73%)
  blocking collectives  138 us (23%)
  between operations  15.6 us (3%)
  matrix products  7.14 us (1%)
    reduce_scatter x1, waiting for transfers between devices, body(): lax.psum_scatter(lax.dot_general(columns, out_grads, (((0,), (0,)), ((),...  321 us
    psum x1, blocking collectives, body(): summed = lax.psum(partial_value, 'mp')  138 us
    all_gather x1, waiting for transfers between devices, body(): lax.all_gather(direction, 'dp', axis=0, tiled=True)  122 us
  transfers between devices with their start and end apart: 3, of which 2 were waited for; matrix products, arithmetic and copies ran while one was open for 1% of the time, Pallas kernels for 0%

commit v1 on v0

v1 whole, which is shorter than its diff:
```python
import jax
import jax.numpy as jnp
from jax import lax
from jax.experimental import pallas as pl
from jax.experimental.pallas import tpu as pltpu
from jax.sharding import PartitionSpec as P

STEP = 10

beta_first = 0.9
beta_second = 0.95
adam_eps = 1e-08
galore_scale = 0.25

NX, NY, NZ = 8, 4, 8
RANK = 1024
TOK = 256
FF = 896
CHUNK = RANK // NX
ROWS = 16
XF = 512
YF = FF - XF
OFFSETS = (4, 3, 5, 2, 6, 1, 7)
NEAR = (1, 7, 2, 6, 3, 5, 4)

f32, bf16 = jnp.float32, jnp.bfloat16

names = (
    ("reduce_z", NZ), ("pair_h", 1), ("gather_z", NZ), ("pair_core", NX), ("first_x", NX), ("first_y", NY * NX),
    ("second_y", NY), ("second_x", NX), ("dir_x", NX), ("dir_y", NY), ("all_y", NY), ("all_x", NX),
    ("core_one", NY), ("core_two", NX), ("rows_h", 1), ("rows_z", NZ),
)
BASE, SEMS = {}, 0
for name, count in names:
    BASE[name] = SEMS
    SEMS += count


def kernel(
    act, grads, basis, first, second, step_out, first_out, second_out,
    part_send, part_recv, half, half_recv, turned, turned_recv, full, core_recv, mine, x_send, x_recv,
    y_send, y_recv, t_send, t_recv, u_send, u_recv, dir_one, dir_two, rows, send, recv,
):
    dp, mp = lax.axis_index("dp"), lax.axis_index("mp")
    x, y, c = dp // (2 * NY), dp // 2 % NY, dp % 2
    z, h = mp // 2, mp % 2

    def at_x(k):
        return (((x + k) % NX * NY + y) * 2 + c, mp)

    def at_y(k):
        return ((x * NY + (y + k) % NY) * 2 + c, mp)

    def at_z(k):
        return (dp, (z + k) % NZ * 2 + h)

    at_h = (dp, z * 2 + 1 - h)
    at_core = (dp + 1 - 2 * c, mp)

    def move(source, target, name, place, device, recv_place=None):
        recv_place = place if recv_place is None else recv_place
        return pltpu.make_async_remote_copy(
            src_ref=source, dst_ref=target, send_sem=send.at[BASE[name] + place],
            recv_sem=recv.at[BASE[name] + recv_place], device_id=device, device_id_type=pl.DeviceIdType.MESH,
        )

    barrier = pltpu.get_barrier_semaphore()
    partners = [at_x(k) for k in range(1, NX)] + [at_y(k) for k in range(1, NY)] + [at_z(k) for k in range(1, NZ)]
    partners += [at_h, at_core]
    for device in partners:
        pl.semaphore_signal(barrier, inc=1, device_id=device, device_id_type=pl.DeviceIdType.MESH)

    holds = z == x
    owns = jnp.logical_and(holds, h == y // 2)

    @pl.when(owns)
    def _():
        rows[...] = basis[pl.ds(pl.multiple_of((y % 2 * 2 + c) * 128, 128), 128), :]

    def rows_h():
        return move(rows, rows, "rows_h", 0, at_h)

    def rows_z(k):
        return move(rows, rows, "rows_z", k, at_z(k), 0)

    def columns(k):
        return pl.ds(pl.multiple_of((z + k + x) % NX * CHUNK, CHUNK), CHUNK)

    def project(k):
        return jnp.dot(act[...], basis[:, columns(k)], preferred_element_type=f32)

    part_send[OFFSETS[0]] = project(OFFSETS[0]).astype(bf16)
    pl.semaphore_wait(barrier, len(partners))
    copies = []
    for k in OFFSETS:
        if k != OFFSETS[0]:
            part_send[k] = project(k).astype(bf16)
        copy = move(part_send.at[k], part_recv.at[k], "reduce_z", k, at_z(k))
        copy.start()
        copies.append(copy)

    @pl.when(owns)
    def _():
        rows_h().start()

    total = project(0)
    for copy, k in zip(copies, OFFSETS):
        copy.wait()
    for k in range(1, NZ):
        total = total + part_recv[k].astype(f32)
    half[...] = total
    copy = move(half, half_recv, "pair_h", 0, at_h)
    copy.start()
    copy.wait()
    turned[...] = jnp.transpose(half[...] + half_recv[...]).astype(bf16)

    gathers = {}
    for k in OFFSETS:
        gathers[k] = move(turned, turned_recv.at[k], "gather_z", k, at_z(k))
        gathers[k].start()

    def away(k):
        return (z - k + NZ) % NX

    def to_core(k):
        return move(full.at[k, :, 1 - c], core_recv.at[k], "pair_core", k, at_core)

    def to_x(o):
        return move(x_send.at[o], x_recv.at[o], "first_x", o, at_x(o))

    def to_y(q, o):
        return move(y_send.at[o, (y + q) % NY], y_recv.at[q, o], "first_y", q * NX + o, at_y(q))

    def sum_cores(k):
        to_core(k).wait_recv()
        o = away(k)
        both = full[k, :, c] + core_recv[k]
        mine[o] = both
        x_send[o] = both[:, :, :XF].astype(bf16)
        y_send[o] = both[:, :, XF:].astype(bf16)

        @pl.when(o != 0)
        def _():
            to_x(o).start()

        for q in range(1, NY):
            to_y(q, o).start()

    order = (0,) + NEAR
    for place, k in enumerate(order):
        if k:
            gathers[k].wait_recv()
            block = turned_recv[k]
        else:
            block = turned[...]
        product = jnp.dot(block, grads[...], preferred_element_type=f32)
        full[k] = product.reshape(NY, 2, ROWS, FF)
        to_core(k).start()
        if place:
            sum_cores(order[place - 1])
    sum_cores(order[-1])

    @pl.when(jnp.logical_and(holds, jnp.logical_not(owns)))
    def _():
        rows_h().wait_recv()

    @pl.when(holds)
    def _():
        for k in OFFSETS:
            rows_z(k).start()

    second_x, second_y = [], []
    for o in range(NX):
        for q in range(1, NY):
            to_y(q, o).wait_recv()
        value = mine[o, y][:, XF:]
        for q in range(1, NY):
            value = value + y_recv[q, o].astype(f32)
        u_send[o] = value
        if o:
            copy = move(u_send.at[o], u_recv.at[o], "second_x", o, at_x(o))
            copy.start()
            second_x.append(copy)
    for o in range(1, NX):
        to_x(o).wait_recv()
    value = mine[0][:, :, :XF]
    for o in range(1, NX):
        value = value + x_recv[o].astype(f32)
    t_send[...] = value
    for q in range(1, NY):
        copy = move(t_send.at[(y + q) % NY], t_recv.at[q], "second_y", q, at_y(q))
        copy.start()
        second_y.append(copy)

    def adam(gradient, columns, target):
        new_first = beta_first * first[:, columns] + (1.0 - beta_first) * gradient
        new_second = beta_second * second[:, columns] + (1.0 - beta_second) * gradient * gradient
        first_hat = new_first / (1.0 - beta_first**STEP)
        second_hat = new_second / (1.0 - beta_second**STEP)
        first_out[:, columns] = new_first
        second_out[:, columns] = new_second
        target[x, y, c] = (first_hat / (jnp.sqrt(second_hat) + adam_eps)).astype(bf16)

    dir_x, dir_y, all_x, all_y, core_one, core_two = [], [], [], [], [], []
    for copy in second_x:
        copy.wait_recv()
    value = u_send[0]
    for o in range(1, NX):
        value = value + u_recv[o]
    adam(value, slice(XF, FF), dir_two)
    for q in range(1, NY):
        copy = move(dir_two.at[x, y, c], dir_two.at[x, y, c], "dir_y", q, at_y(q))
        copy.start()
        dir_y.append(copy)
    for copy in second_y:
        copy.wait_recv()
    value = t_send[y]
    for q in range(1, NY):
        value = value + t_recv[q]
    adam(value, slice(0, XF), dir_one)
    for o in OFFSETS:
        copy = move(dir_one.at[x, y, c], dir_one.at[x, y, c], "dir_x", o, at_x(o))
        copy.start()
        dir_x.append(copy)

    def core_rows_one(q):
        block = dir_one.at[:, (y + NY - q) % NY, c]
        return move(block, block, "core_one", q, at_core)

    def core_rows_two(o):
        block = dir_two.at[(x + NX - o) % NX, :, c]
        return move(block, block, "core_two", o, at_core)

    for copy in dir_y:
        copy.wait_recv()
    for o in OFFSETS:
        copy = move(dir_two.at[x, :, c], dir_two.at[x, :, c], "all_x", o, at_x(o))
        copy.start()
        all_x.append(copy)
    core_two.append(core_rows_two(0))
    core_two[-1].start()
    for copy in dir_x:
        copy.wait_recv()
    for q in range(1, NY):
        copy = move(dir_one.at[:, y, c], dir_one.at[:, y, c], "all_y", q, at_y(q))
        copy.start()
        all_y.append(copy)
    core_one.append(core_rows_one(0))
    core_one[-1].start()
    by_offset = dict(zip(OFFSETS, all_x))
    for o in NEAR:
        by_offset[o].wait_recv()
        core_two.append(core_rows_two(o))
        core_two[-1].start()
    for q in (1, 3, 2):
        all_y[q - 1].wait_recv()
        core_one.append(core_rows_one(q))
        core_one[-1].start()

    @pl.when(jnp.logical_not(holds))
    def _():
        rows_z(0).wait_recv()

    for copy in core_two:
        copy.wait_recv()
    step_out[:, XF:] = galore_scale * jnp.dot(
        rows[...], dir_two[...].reshape(RANK, YF), preferred_element_type=f32
    )
    for copy in core_one:
        copy.wait_recv()
    step_out[:, :XF] = galore_scale * jnp.dot(
        rows[...], dir_one[...].reshape(RANK, XF), preferred_element_type=f32
    )

    for k in OFFSETS:
        gathers[k].wait_send()
    for k in range(NX):
        to_core(k).wait_send()
    for o in range(NX):
        if o:
            to_x(o).wait_send()
        for q in range(1, NY):
            to_y(q, o).wait_send()
    for copy in second_x + second_y + dir_x + dir_y + all_x + all_y + core_one + core_two:
        copy.wait_send()

    @pl.when(owns)
    def _():
        rows_h().wait_send()

    @pl.when(holds)
    def _():
        for k in OFFSETS:
            rows_z(k).wait_send()


def body(activations, out_grads, basis, first_moment, second_moment):
    vmem = pl.BlockSpec(memory_space=pltpu.VMEM)
    return pl.pallas_call(
        kernel,
        out_shape=(
            jax.ShapeDtypeStruct((128, FF), f32),
            jax.ShapeDtypeStruct((ROWS, FF), f32),
            jax.ShapeDtypeStruct((ROWS, FF), f32),
        ),
        in_specs=[vmem] * 5,
        out_specs=(vmem,) * 3,
        scratch_shapes=[
            pltpu.VMEM((NZ, TOK, CHUNK), bf16),
            pltpu.VMEM((NZ, TOK, CHUNK), bf16),
            pltpu.VMEM((TOK, CHUNK), f32),
            pltpu.VMEM((TOK, CHUNK), f32),
            pltpu.VMEM((CHUNK, TOK), bf16),
            pltpu.VMEM((NZ, CHUNK, TOK), bf16),
            pltpu.VMEM((NX, NY, 2, ROWS, FF), f32),
            pltpu.VMEM((NX, NY, ROWS, FF), f32),
            pltpu.VMEM((NX, NY, ROWS, FF), f32),
            pltpu.VMEM((NX, NY, ROWS, XF), bf16),
            pltpu.VMEM((NX, NY, ROWS, XF), bf16),
            pltpu.VMEM((NX, NY, ROWS, YF), bf16),
            pltpu.VMEM((NY, NX, ROWS, YF), bf16),
            pltpu.VMEM((NY, ROWS, XF), f32),
            pltpu.VMEM((NY, ROWS, XF), f32),
            pltpu.VMEM((NX, ROWS, YF), f32),
            pltpu.VMEM((NX, ROWS, YF), f32),
            pltpu.VMEM((NX, NY, 2, ROWS, XF), bf16),
            pltpu.VMEM((NX, NY, 2, ROWS, YF), bf16),
            pltpu.VMEM((128, RANK), bf16),
            pltpu.SemaphoreType.DMA((SEMS,)),
            pltpu.SemaphoreType.DMA((SEMS,)),
        ],
        compiler_params=pltpu.CompilerParams(
            collective_id=0, has_side_effects=True, vmem_limit_bytes=40 << 20
        ),
        cost_estimate=pl.CostEstimate(flops=10**9, bytes_accessed=4 << 20, transcendentals=0),
        name="galore_step",
    )(activations, out_grads, basis, first_moment, second_moment)


def solution(mesh):
    return jax.shard_map(
        body,
        mesh=mesh,
        in_specs=(P("dp", "mp"), P("dp", "mp"), P("mp", None), P("dp", "mp"), P("dp", "mp")),
        out_specs=(P("dp", "mp"), P("dp", "mp"), P("dp", "mp")),
        check_vma=False,
    )
```

time: 608 us -> 106 us (0.17)
  waiting for transfers between devices: 443 us -> 0 us
  blocking collectives: 138 us -> 0 us
  Pallas kernels: 0 us -> 97.9 us
  between operations: 15.6 us -> 0.65 us
  matrix products: 7.14 us -> 0 us
  local copies, waits for them, and re-layouts: 0.02 us -> 6.84 us
    reduce_scatter x1 -> x0, waiting for transfers between devices: 321 us -> none  [body(): lax.psum_scatter(lax.dot_general(columns, out_grads, (((0,), (0,)), ((),...]
    psum x1 -> x0, blocking collectives: 138 us -> none  [body(): summed = lax.psum(partial_value, 'mp')]
    all_gather x1 -> x0, waiting for transfers between devices: 122 us -> none  [body(): lax.all_gather(direction, 'dp', axis=0, tiled=True)]
    pallas_call x0 -> x1, Pallas kernels: none -> 97.9 us  [body(): pl.pallas_call(kernel, out_shape=(jax.ShapeDtypeStruct((128, FF), f32), j...]
    dot_general x3 -> x0, matrix products: 7.14 us -> none  [the longest x1 2.82 us: body(): jnp.dot(columns, lax.all_gather(direction, 'dp', axis=0, tiled=True), pre...]
    unnamed x6 -> x13, local copies, waits for them, and re-layouts: 0.02 us -> 6.84 us
  transfers between devices with their start and end apart: 3 -> 0, of which waited for: 2 -> 0; matrix products, arithmetic and copies ran while one was open for 1% -> 0% of each run, Pallas kernels for 0% -> 0%
where the time goes in v1:
time: 106 us; the launch traced here: 105 us
  Pallas kernels  97.9 us (92%)
  local copies, waits for them, and re-layouts  6.84 us (6%)
    pallas_call x1, Pallas kernels, body(): pl.pallas_call(kernel, out_shape=(jax.ShapeDtypeStruct((128, FF), f32), j...  97.9 us
    unnamed x13, local copies, waits for them, and re-layouts  6.84 us

profile of v1, /device:TPU:1, one launch (start us, length us, event | category | flops | bytes accessed | tf_op | source)
XLA Modules:
  0.0 105.4 jit_solution(2744970941488349076)
XLA Ops:
  0.6 0.0 copy-start
  0.6 1.2 %copy-done = bf16[512,1024]{1,0:T(8,128)(2,1)S(1)} copy-done((bf16[512,1024]{1,0:T(8,128)(2,1)S(1)}, bf16[512,1024]{1,0:T(8,128)(2,1)}, u32[]{:S(2)}) %copy-start) | copy-done | bytes 1048600
  1.9 0.0 copy-start.1
  1.9 1.0 copy-done.1
  2.9 0.0 copy-start.2
  2.9 0.9 copy-done.2
  3.8 0.0 copy-start.3
  3.8 0.8 copy-done.3
  4.6 0.0 copy-start.4
  4.6 0.8 copy-done.4
  5.5 97.9 %galore_step.1 = (f32[128,896]{1,0:T(8,128)S(1)}, f32[16,896]{1,0:T(8,128)S(1)}, f32[16,896]{1,0:T(8,128)S(1)}) custom-call(bf16[256,512]{1,0:T(8,128)(2,1)S(1)} %copy-done.2, bf16[256,896]{1,0:T(8,128)(2,1)S(1)} %copy-done.1, bf16[512,1024]{1,0:T(8,128)(2,1)S(1)} %copy-done, f32[16,896]{1,0:T(8,128)S(1)} %copy-done.3, f32[16,896]{1,0:T(8,128)S(1)} %copy-done.4), custom_call_target="tpu_custom_call" | custom-call | flops 1000000000 | bytes 4194304 | tf_op jit(solution)/shard_map/galore_step/pallas_call | solution.py:299
  103.4 0.8 copy.11
  104.2 0.6 copy.12
  104.8 0.6 copy.13
Async XLA Ops:
  0.6 1.2 %copy-start = (bf16[512,1024]{1,0:T(8,128)(2,1)S(1)}, bf16[512,1024]{1,0:T(8,128)(2,1)}, u32[]{:S(2)}) copy-start(bf16[512,1024]{1,0:T(8,128)(2,1)} %basis.1) | copy-start | bytes 3145732
  1.9 1.0 copy-start.1
  2.9 0.9 copy-start.2
  3.8 0.8 copy-start.3
  4.6 0.8 copy-start.4

commit v2 on v1

v2 whole, which is shorter than its diff:
```python
import jax
import jax.numpy as jnp
from jax import lax
from jax.experimental import pallas as pl
from jax.experimental.pallas import tpu as pltpu
from jax.sharding import PartitionSpec as P

STEP = 10

beta_first = 0.9
beta_second = 0.95
adam_eps = 1e-08
galore_scale = 0.25

NX, NY, NZ = 8, 4, 8
RANK = 1024
TOK = 256
FF = 896
CHUNK = RANK // NX
PARTS = 2
PART = CHUNK // PARTS
PART_Y = NY // PARTS
BEHIND = 3
ROWS = 16
XF = 384
YF = FF - XF
OFFSETS = (4, 3, 5, 2, 6, 1, 7)
NEAR = (1, 7, 2, 6, 3, 5, 4)
SIDES = (1, 3, 2)

f32, bf16 = jnp.float32, jnp.bfloat16

names = (
    ("reduce_z", PARTS * NZ), ("pair_h", PARTS), ("gather_z", PARTS * NZ), ("pair_core", PARTS * NX),
    ("first_x", PARTS * NX), ("first_y", NY * NX),
    ("second_y", NY), ("second_x", NX), ("one", NY * NX), ("two", NY * NX), ("core_one", NY * NX),
    ("core_two", NY * NX), ("rows_h", 1), ("rows_z", NZ),
)
BASE, SEMS = {}, 0
for name, count in names:
    BASE[name] = SEMS
    SEMS += count


def kernel(
    act_in, grads_in, basis_in, first_in, second_in, step_out, first_out, second_out,
    act, grads, basis, first, second,
    own, part_send, part_recv, half, half_recv, turned, turned_recv, full, core_recv, mine, x_send, x_recv,
    y_send, y_recv, t_send, t_recv, u_send, u_recv, dir_one, dir_two, rows, send, recv, load,
):
    dp, mp = lax.axis_index("dp"), lax.axis_index("mp")
    x, y, c = dp // (2 * NY), dp // 2 % NY, dp % 2
    z, h = mp // 2, mp % 2

    def at_x(k):
        return (((x + k) % NX * NY + y) * 2 + c, mp)

    def at_y(k):
        return ((x * NY + (y + k) % NY) * 2 + c, mp)

    def at_z(k):
        return (dp, (z + k) % NZ * 2 + h)

    at_h = (dp, z * 2 + 1 - h)
    at_core = (dp + 1 - 2 * c, mp)

    def move(source, target, name, place, device, recv_place=None):
        recv_place = place if recv_place is None else recv_place
        return pltpu.make_async_remote_copy(
            src_ref=source, dst_ref=target, send_sem=send.at[BASE[name] + place],
            recv_sem=recv.at[BASE[name] + recv_place], device_id=device, device_id_type=pl.DeviceIdType.MESH,
        )

    loads = []
    for i, (source, target) in enumerate(
        ((act_in, act), (basis_in, basis), (grads_in, grads), (first_in, first), (second_in, second))
    ):
        loads.append(pltpu.make_async_copy(source, target, load.at[i]))
        loads[-1].start()

    pending = []

    def finish():
        for wait in pending:
            wait()

    def go(copy):
        copy.start()
        pending.append(copy.wait_send)
        return copy

    barrier = pltpu.get_barrier_semaphore()
    partners = [at_x(k) for k in range(1, NX)] + [at_y(k) for k in range(1, NY)] + [at_z(k) for k in range(1, NZ)]
    partners += [at_h, at_core]
    for device in partners:
        pl.semaphore_signal(barrier, inc=1, device_id=device, device_id_type=pl.DeviceIdType.MESH)

    holds = z == x
    owns = jnp.logical_and(holds, h == y // 2)

    loads[0].wait()
    loads[1].wait()

    @pl.when(owns)
    def _():
        rows[...] = basis[pl.ds(pl.multiple_of((y % 2 * 2 + c) * 128, 128), 128), :]

    def rows_h():
        return move(rows, rows, "rows_h", 0, at_h)

    def rows_z(k):
        return move(rows, rows, "rows_z", k, at_z(k), 0)

    def columns(k):
        return pl.ds(pl.multiple_of((z + k + x) % NX * CHUNK, CHUNK), CHUNK)

    def project(k):
        return jnp.transpose(jnp.dot(act[...], basis[:, columns(k)], preferred_element_type=f32))

    def reduce_z(p, k):
        return move(part_send.at[p, k], part_recv.at[p, k], "reduce_z", p * NZ + k, at_z(k))

    for i, k in enumerate(OFFSETS):
        value = project(k).astype(bf16)
        for p in range(PARTS):
            part_send[p, k] = value[p * PART : (p + 1) * PART]
        if i == 0:
            pl.semaphore_wait(barrier, len(partners))
        go(reduce_z(0, k))
    for p in range(1, PARTS):
        for k in OFFSETS:
            go(reduce_z(p, k))

    @pl.when(owns)
    def _():
        rows_h().start()

    def sent_rows_h():
        @pl.when(owns)
        def _():
            rows_h().wait_send()

    pending.append(sent_rows_h)
    own[...] = project(0)
    pairs = []
    for p in range(PARTS):
        total = own[p * PART : (p + 1) * PART, :]
        for k in OFFSETS:
            reduce_z(p, k).wait_recv()
        for k in range(1, NZ):
            total = total + part_recv[p, k].astype(f32)
        half[p] = total
        pairs.append(go(move(half.at[p], half_recv.at[p], "pair_h", p, at_h)))

    def gather_z(p, k):
        ranks = pl.ds(p * PART, PART)
        return move(turned.at[ranks], turned_recv.at[k, ranks], "gather_z", p * NZ + k, at_z(k))

    def gather(p):
        pairs[p].wait_recv()
        turned[pl.ds(p * PART, PART), :] = (half[p] + half_recv[p]).astype(bf16)
        for k in NEAR:
            go(gather_z(p, k))

    def away(k):
        return (z - k + NZ) % NX

    def ys(p):
        return pl.ds(p * PART_Y, PART_Y)

    def to_core(p, k):
        return move(full.at[k, ys(p), 1 - c], core_recv.at[k, ys(p)], "pair_core", p * NX + k, at_core)

    def to_x(p, o):
        return move(x_send.at[o, ys(p)], x_recv.at[o, ys(p)], "first_x", p * NX + o, at_x(o))

    def to_y(q, o):
        return move(y_send.at[o, (y + q) % NY], y_recv.at[q, o], "first_y", q * NX + o, at_y(q))

    def sum_cores(p, k):
        to_core(p, k).wait_recv()
        o = away(k)
        both = full[k, ys(p), c] + core_recv[k, ys(p)]
        mine[o, ys(p)] = both
        x_send[o, ys(p)] = both[:, :, :XF].astype(bf16)
        y_send[o, ys(p)] = both[:, :, XF:].astype(bf16)

        @pl.when(o != 0)
        def _():
            to_x(p, o).start()

        for i in range(PART_Y):
            q = (p * PART_Y + i - y + NY) % NY

            @pl.when(q != 0)
            def _():
                to_y(q, o).start()

    def gradient(p, k):
        if k:
            gather_z(p, k).wait_recv()
            block = turned_recv[k, pl.ds(p * PART, PART)]
        else:
            block = turned[pl.ds(p * PART, PART), :]
        product = jnp.dot(block, grads[...], preferred_element_type=f32)
        full[k, ys(p)] = product.reshape(PART_Y, 2, ROWS, FF)
        go(to_core(p, k))

    loads[2].wait()
    work = [(p, k) for p in range(PARTS) for k in (0,) + NEAR]
    gather(0)
    for i, (p, k) in enumerate(work):
        gradient(p, k)
        if i % NZ == 0 and p + 1 < PARTS:
            gather(p + 1)
        if i >= BEHIND:
            sum_cores(*work[i - BEHIND])
    for item in work[len(work) - BEHIND :]:
        sum_cores(*item)
    for o in range(NX):
        if o:
            for p in range(PARTS):
                pending.append(to_x(p, o).wait_send)
        for q in range(1, NY):
            pending.append(to_y(q, o).wait_send)

    @pl.when(jnp.logical_and(holds, jnp.logical_not(owns)))
    def _():
        rows_h().wait_recv()

    @pl.when(holds)
    def _():
        for k in OFFSETS:
            rows_z(k).start()

    def sent_rows_z():
        @pl.when(holds)
        def _():
            for k in OFFSETS:
                rows_z(k).wait_send()

    pending.append(sent_rows_z)

    def second_x(o):
        return move(u_send.at[o], u_recv.at[o], "second_x", o, at_x(o))

    def sum_y(o):
        value = mine[o, y][:, XF:]
        for q in range(1, NY):
            value = value + y_recv[q, o].astype(f32)
        return value

    for k in (0,) + NEAR:
        o = away(k)
        for q in range(1, NY):
            to_y(q, o).wait_recv()
        u_send[o] = sum_y(o).astype(bf16)

        @pl.when(o != 0)
        def _():
            second_x(o).start()

    for o in range(1, NX):
        pending.append(second_x(o).wait_send)
    value = mine[0][:, :, :XF]
    for o in range(1, NX):
        for p in range(PARTS):
            to_x(p, o).wait_recv()
        value = value + x_recv[o].astype(f32)
    t_send[...] = value
    second_y = []
    for q in SIDES:
        second_y.append(go(move(t_send.at[(y + q) % NY], t_recv.at[q], "second_y", q, at_y(q))))

    loads[3].wait()
    loads[4].wait()

    def adam(gradient, columns, target):
        new_first = beta_first * first[:, columns] + (1.0 - beta_first) * gradient
        new_second = beta_second * second[:, columns] + (1.0 - beta_second) * gradient * gradient
        first_hat = new_first / (1.0 - beta_first**STEP)
        second_hat = new_second / (1.0 - beta_second**STEP)
        first_out[:, columns] = new_first
        second_out[:, columns] = new_second
        target[x, y, c] = (first_hat / (jnp.sqrt(second_hat) + adam_eps)).astype(bf16)

    def block(q, o):
        return (x + NX - o) % NX, (y + NY - q) % NY, c

    def to_x_one(o):
        ref = dir_one.at[x, y, c]
        return move(ref, ref, "one", o, at_x(o))

    def to_y_one(q, o):
        ref = dir_one.at[block(0, o)]
        return move(ref, ref, "one", q * NX + o, at_y(q))

    def to_y_two(q):
        ref = dir_two.at[x, y, c]
        return move(ref, ref, "two", q * NX, at_y(q))

    def to_x_two(q, o):
        ref = dir_two.at[block(q, 0)]
        return move(ref, ref, "two", q * NX + o, at_x(o))

    def share(array, name, q, o):
        ref = array.at[block(q, o)]
        return move(ref, ref, name, q * NX + o, at_core)

    def came(array, name, q, o):
        ref = array.at[block(q, o)]
        move(ref, ref, name, q * NX + o, at_x(1)).wait_recv()

    for copy in second_y:
        copy.wait_recv()
    value = t_send[y]
    for q in range(1, NY):
        value = value + t_recv[q]
    adam(value, slice(0, XF), dir_two)
    for q in SIDES:
        go(to_y_two(q))
    for o in OFFSETS:
        go(to_x_two(0, o))
    go(share(dir_two, "core_two", 0, 0))
    value = sum_y(0)
    for o in range(1, NX):
        second_x(o).wait_recv()
        value = value + u_recv[o].astype(f32)
    adam(value, slice(XF, FF), dir_one)
    for o in OFFSETS:
        go(to_x_one(o))
    for q in SIDES:
        go(to_y_one(q, 0))
    go(share(dir_one, "core_one", 0, 0))
    for q in SIDES:
        came(dir_two, "two", q, 0)
        for o in OFFSETS:
            go(to_x_two(q, o))
        go(share(dir_two, "core_two", q, 0))
    for o in NEAR:
        came(dir_one, "one", 0, o)
        for q in SIDES:
            go(to_y_one(q, o))
        go(share(dir_one, "core_one", 0, o))
    for q in (0,) + SIDES:
        for o in NEAR:
            came(dir_two, "two", q, o)
            go(share(dir_two, "core_two", q, o))
    for o in (0,) + NEAR:
        for q in SIDES:
            came(dir_one, "one", q, o)
            go(share(dir_one, "core_one", q, o))

    @pl.when(jnp.logical_not(holds))
    def _():
        rows_z(0).wait_recv()

    for q in range(NY):
        for o in range(NX):
            share(dir_two, "core_two", q, o).wait_recv()
    step_out[:, :XF] = galore_scale * jnp.dot(
        rows[...], dir_two[...].reshape(RANK, XF), preferred_element_type=f32
    )
    for q in range(NY):
        for o in range(NX):
            share(dir_one, "core_one", q, o).wait_recv()
    step_out[:, XF:] = galore_scale * jnp.dot(
        rows[...], dir_one[...].reshape(RANK, YF), preferred_element_type=f32
    )
    finish()


def body(activations, out_grads, basis, first_moment, second_moment):
    vmem = pl.BlockSpec(memory_space=pltpu.VMEM)
    return pl.pallas_call(
        kernel,
        out_shape=(
            jax.ShapeDtypeStruct((128, FF), f32),
            jax.ShapeDtypeStruct((ROWS, FF), f32),
            jax.ShapeDtypeStruct((ROWS, FF), f32),
        ),
        in_specs=[pl.BlockSpec(memory_space=pl.ANY)] * 5,
        out_specs=(vmem,) * 3,
        scratch_shapes=[
            pltpu.VMEM((TOK, 512), bf16),
            pltpu.VMEM((TOK, FF), bf16),
            pltpu.VMEM((512, RANK), bf16),
            pltpu.VMEM((ROWS, FF), f32),
            pltpu.VMEM((ROWS, FF), f32),
            pltpu.VMEM((CHUNK, TOK), f32),
            pltpu.VMEM((PARTS, NZ, PART, TOK), bf16),
            pltpu.VMEM((PARTS, NZ, PART, TOK), bf16),
            pltpu.VMEM((PARTS, PART, TOK), f32),
            pltpu.VMEM((PARTS, PART, TOK), f32),
            pltpu.VMEM((CHUNK, TOK), bf16),
            pltpu.VMEM((NZ, CHUNK, TOK), bf16),
            pltpu.VMEM((NX, NY, 2, ROWS, FF), f32),
            pltpu.VMEM((NX, NY, ROWS, FF), f32),
            pltpu.VMEM((NX, NY, ROWS, FF), f32),
            pltpu.VMEM((NX, NY, ROWS, XF), bf16),
            pltpu.VMEM((NX, NY, ROWS, XF), bf16),
            pltpu.VMEM((NX, NY, ROWS, YF), bf16),
            pltpu.VMEM((NY, NX, ROWS, YF), bf16),
            pltpu.VMEM((NY, ROWS, XF), f32),
            pltpu.VMEM((NY, ROWS, XF), f32),
            pltpu.VMEM((NX, ROWS, YF), bf16),
            pltpu.VMEM((NX, ROWS, YF), bf16),
            pltpu.VMEM((NX, NY, 2, ROWS, YF), bf16),
            pltpu.VMEM((NX, NY, 2, ROWS, XF), bf16),
            pltpu.VMEM((128, RANK), bf16),
            pltpu.SemaphoreType.DMA((SEMS,)),
            pltpu.SemaphoreType.DMA((SEMS,)),
            pltpu.SemaphoreType.DMA((5,)),
        ],
        compiler_params=pltpu.CompilerParams(
            collective_id=0, has_side_effects=True, vmem_limit_bytes=60 << 20
        ),
        cost_estimate=pl.CostEstimate(flops=10**9, bytes_accessed=4 << 20, transcendentals=0),
        name="galore_step",
    )(activations, out_grads, basis, first_moment, second_moment)


def solution(mesh):
    return jax.shard_map(
        body,
        mesh=mesh,
        in_specs=(P("dp", "mp"), P("dp", "mp"), P("mp", None), P("dp", "mp"), P("dp", "mp")),
        out_specs=(P("dp", "mp"), P("dp", "mp"), P("dp", "mp")),
        check_vma=False,
    )
```

time: 106 us -> 94.7 us (0.89)
  Pallas kernels: 97.9 us -> 90.5 us
  local copies, waits for them, and re-layouts: 6.84 us -> 3.3 us
    pallas_call x1, Pallas kernels: 97.9 us -> 90.5 us  [body(): pl.pallas_call(kernel, out_shape=(jax.ShapeDtypeStruct((128, FF), f32), j...]
    unnamed x13 -> x7, local copies, waits for them, and re-layouts: 6.84 us -> 3.3 us
where the time goes in v2:
time: 94.7 us; the launch traced here: 94.4 us
  Pallas kernels  90.5 us (96%)
  local copies, waits for them, and re-layouts  3.3 us (3%)
    pallas_call x1, Pallas kernels, body(): pl.pallas_call(kernel, out_shape=(jax.ShapeDtypeStruct((128, FF), f32), j...  90.5 us
    unnamed x7, local copies, waits for them, and re-layouts  3.3 us

profile of v2, /device:TPU:1, one launch (start us, length us, event | category | flops | bytes accessed | tf_op | source)
XLA Modules:
  0.0 94.4 jit_solution(16108794517993562566)
XLA Ops:
  0.6 90.5 %galore_step.1 = (f32[128,896]{1,0:T(8,128)}, f32[16,896]{1,0:T(8,128)}, f32[16,896]{1,0:T(8,128)}) custom-call(bf16[256,512]{1,0:T(8,128)(2,1)} %act_in.1, bf16[256,896]{1,0:T(8,128)(2,1)} %grads_in.1, bf16[512,1024]{1,0:T(8,128)(2,1)} %basis_in.1, f32[16,896]{1,0:T(8,128)} %first_in.1, f32[16,896]{1,0:T(8,128)} %second_in.1), custom_call_target="tpu_custom_call" | custom-call | flops 1000000000 | bytes 4194304 | tf_op jit(solution)/shard_map/galore_step/pallas_call | solution.py:375
  91.1 0.0 copy-start.1
  91.1 1.8 %copy.11 = f32[128,896]{1,0:T(8,128)} copy(f32[128,896]{1,0:T(8,128)} %get-tuple-element.6) | data formatting | bytes 917504
  93.0 0.0 copy-done.1
  93.0 0.0 copy-start
  93.0 0.6 copy.12
  93.6 0.2 copy-done
  93.8 0.6 copy.13
Async XLA Ops:
  91.1 1.8 %copy-start.1 = (f32[16,896]{1,0:T(8,128)S(1)}, f32[16,896]{1,0:T(8,128)}, u32[]{:S(2)}) copy-start(f32[16,896]{1,0:T(8,128)} %get-tuple-element.7) | copy-start | bytes 172036
  93.0 0.8 copy-start

commit v3 on v2

v3 whole, which is shorter than its diff:
```python
import jax
import jax.numpy as jnp
from jax import lax
from jax.experimental import pallas as pl
from jax.experimental.pallas import tpu as pltpu
from jax.sharding import PartitionSpec as P

STEP = 10

beta_first = 0.9
beta_second = 0.95
adam_eps = 1e-08
galore_scale = 0.25

NX, NY, NZ = 8, 4, 8
RANK = 1024
TOK = 256
FF = 896
CHUNK = RANK // NX
PARTS = 2
PART = CHUNK // PARTS
PART_Y = NY // PARTS
BEHIND = 3
ROWS = 16
XF = 384
YF = FF - XF
OFFSETS = (4, 3, 5, 2, 6, 1, 7)
NEAR = (1, 7, 2, 6, 3, 5, 4)
SIDES = (1, 3, 2)

f32, bf16 = jnp.float32, jnp.bfloat16

EXCHANGES = {
    "reduce_z": (1, PARTS), "pair_h": (1, PARTS), "gather_z": (1, PARTS * NZ), "pair_core": (1, PARTS * NX),
    "first_x": (1, 1), "first_y": (1, NX), "second_y": (1, 1), "second_x": (1, 1),
    "x_one": (1, NX), "y_one": (1, NX), "y_two": (1, NY), "x_two": (1, NX), "core_one": (1, 1), "core_two": (1, 1),
    "rows_h": (1, 1), "rows_z": (2, 1),
}
SENDS, RECVS, BASE = 0, 0, {}
for name, (sends, recvs) in EXCHANGES.items():
    BASE[name] = (SENDS, RECVS)
    SENDS, RECVS = SENDS + sends, RECVS + recvs


def kernel(
    act_in, grads_in, basis_in, first_in, second_in, step_out, first_out, second_out,
    act, grads, basis, first, second,
    own, part_send, part_recv, half, half_recv, turned, turned_recv, full, core_recv, mine, x_send, x_recv,
    y_send, y_recv, t_send, t_recv, u_send, u_recv, dir_one, dir_two, rows, send, recv, load,
):
    dp, mp = lax.axis_index("dp"), lax.axis_index("mp")
    x, y, c = dp // (2 * NY), dp // 2 % NY, dp % 2
    z, h = mp // 2, mp % 2

    def at_x(k):
        return (((x + k) % NX * NY + y) * 2 + c, mp)

    def at_y(k):
        return ((x * NY + (y + k) % NY) * 2 + c, mp)

    def at_z(k):
        return (dp, (z + k) % NZ * 2 + h)

    at_h = (dp, z * 2 + 1 - h)
    at_core = (dp + 1 - 2 * c, mp)

    def move(source, target, name, device, place=0, send_place=0):
        return pltpu.make_async_remote_copy(
            src_ref=source, dst_ref=target, send_sem=send.at[BASE[name][0] + send_place],
            recv_sem=recv.at[BASE[name][1] + place], device_id=device, device_id_type=pl.DeviceIdType.MESH,
        )

    def arrived(ref, name, place=0):
        move(ref, ref, name, at_core, place).wait_recv()

    def left_here(ref, name):
        pending.append(move(ref, ref, name, at_core).wait_send)

    others = pl.ds(1, NX - 1)
    others_y = pl.ds(1, NY - 1)

    loads = []
    for i, (source, target) in enumerate(
        ((act_in, act), (basis_in, basis), (grads_in, grads), (first_in, first), (second_in, second))
    ):
        loads.append(pltpu.make_async_copy(source, target, load.at[i]))
    loads[0].start()
    loads[1].start()

    pending = []

    def finish():
        for wait in pending:
            wait()

    barrier = pltpu.get_barrier_semaphore()
    partners = [at_x(k) for k in range(1, NX)] + [at_y(k) for k in range(1, NY)] + [at_z(k) for k in range(1, NZ)]
    partners += [at_h, at_core]
    for device in partners:
        pl.semaphore_signal(barrier, inc=1, device_id=device, device_id_type=pl.DeviceIdType.MESH)

    holds = z == x
    owns = jnp.logical_and(holds, h == y // 2)

    loads[0].wait()
    loads[1].wait()

    @pl.when(owns)
    def _():
        rows[...] = basis[pl.ds(pl.multiple_of((y % 2 * 2 + c) * 128, 128), 128), :]

    def rows_h():
        return move(rows, rows, "rows_h", at_h)

    right, left = (z - x + NZ) % NZ, (x - z + NZ) % NZ

    def rows_z(way):
        return move(rows, rows, "rows_z", at_z(1 if way == 0 else NZ - 1), 0, way)

    def pass_rows(step):
        for way, hops in enumerate((right, left)):
            if step < NZ // 2 - way:

                @pl.when(hops == step)
                def _():
                    if step:
                        rows_z(0).wait_recv()
                    rows_z(way).start()

    def columns(k):
        return pl.ds(pl.multiple_of((z + k + x) % NX * CHUNK, CHUNK), CHUNK)

    def project(k):
        return jnp.transpose(jnp.dot(act[...], basis[:, columns(k)], preferred_element_type=f32))

    def reduce_z(p, k):
        return move(part_send.at[p, k], part_recv.at[p, k], "reduce_z", at_z(k), p)

    for i, k in enumerate(OFFSETS):
        value = project(k).astype(bf16)
        for p in range(PARTS):
            part_send[p, k] = value[p * PART : (p + 1) * PART]
        if i == 0:
            pl.semaphore_wait(barrier, len(partners))
        reduce_z(0, k).start()
    for p in range(1, PARTS):
        for k in OFFSETS:
            reduce_z(p, k).start()
    left_here(part_send.at[:, others], "reduce_z")
    for copy in loads[2:]:
        copy.start()

    @pl.when(owns)
    def _():
        rows_h().start()

    def sent_rows_h():
        @pl.when(owns)
        def _():
            rows_h().wait_send()

    pending.append(sent_rows_h)
    def pair_h(p):
        return move(half.at[p], half_recv.at[p], "pair_h", at_h, p)

    own[...] = project(0)
    for p in range(PARTS):
        total = own[p * PART : (p + 1) * PART, :]
        arrived(part_recv.at[p, others], "reduce_z", p)
        for k in range(1, NZ):
            total = total + part_recv[p, k].astype(f32)
        half[p] = total
        pair_h(p).start()
    left_here(half, "pair_h")

    def gather_z(p, k):
        ranks = pl.ds(p * PART, PART)
        return move(turned.at[ranks], turned_recv.at[k, ranks], "gather_z", at_z(k), p * NZ + k)

    def gather(p):
        pair_h(p).wait_recv()
        turned[pl.ds(p * PART, PART), :] = (half[p] + half_recv[p]).astype(bf16)
        for k in NEAR:
            gather_z(p, k).start()

    def away(k):
        return (z - k + NZ) % NX

    def ys(p):
        return pl.ds(p * PART_Y, PART_Y)

    def to_core(p, k):
        return move(full.at[k, ys(p), 1 - c], core_recv.at[k, ys(p)], "pair_core", at_core, p * NX + k)

    def to_x(p, o):
        return move(x_send.at[o, ys(p)], x_recv.at[o, ys(p)], "first_x", at_x(o))

    def to_y(q, o):
        return move(y_send.at[o, (y + q) % NY], y_recv.at[q, o], "first_y", at_y(q), o)

    def sum_cores(p, k):
        to_core(p, k).wait_recv()
        o = away(k)
        both = full[k, ys(p), c] + core_recv[k, ys(p)]
        mine[o, ys(p)] = both
        x_send[o, ys(p)] = both[:, :, :XF].astype(bf16)
        y_send[o, ys(p)] = both[:, :, XF:].astype(bf16)

        @pl.when(o != 0)
        def _():
            to_x(p, o).start()

        for i in range(PART_Y):
            q = (p * PART_Y + i - y + NY) % NY

            @pl.when(q != 0)
            def _():
                to_y(q, o).start()

    def gradient(p, k):
        if k:
            gather_z(p, k).wait_recv()
            block = turned_recv[k, pl.ds(p * PART, PART)]
        else:
            block = turned[pl.ds(p * PART, PART), :]
        product = jnp.dot(block, grads[...], preferred_element_type=f32)
        full[k, ys(p)] = product.reshape(PART_Y, 2, ROWS, FF)
        to_core(p, k).start()

    loads[2].wait()
    work = [(p, k) for p in range(PARTS) for k in (0,) + NEAR]
    gather(0)
    for i, (p, k) in enumerate(work):
        gradient(p, k)
        if i % NZ == 0 and p + 1 < PARTS:
            gather(p + 1)
        if i >= BEHIND:
            sum_cores(*work[i - BEHIND])
    for item in work[len(work) - BEHIND :]:
        sum_cores(*item)
    left_here(turned_recv.at[others], "gather_z")
    left_here(core_recv, "pair_core")
    left_here(x_send.at[others], "first_x")
    left_here(y_recv.at[others_y], "first_y")

    @pl.when(jnp.logical_and(holds, jnp.logical_not(owns)))
    def _():
        rows_h().wait_recv()

    pass_rows(0)

    def sent_rows_z():
        for way, hops in enumerate((right, left)):

            @pl.when(hops < NZ // 2 - way)
            def _():
                rows_z(way).wait_send()

    pending.append(sent_rows_z)

    def second_x(o):
        return move(u_send.at[o], u_recv.at[o], "second_x", at_x(o))

    def sum_y(o):
        value = mine[o, y][:, XF:]
        for q in range(1, NY):
            value = value + y_recv[q, o].astype(f32)
        return value

    for k in (0,) + NEAR:
        o = away(k)
        arrived(y_recv.at[others_y, o], "first_y", o)
        u_send[o] = sum_y(o).astype(bf16)

        @pl.when(o != 0)
        def _():
            second_x(o).start()

    left_here(u_send.at[others], "second_x")
    arrived(x_recv.at[others], "first_x")
    value = mine[0][:, :, :XF]
    for o in range(1, NX):
        value = value + x_recv[o].astype(f32)
    t_send[...] = value
    for q in SIDES:
        move(t_send.at[(y + q) % NY], t_recv.at[q], "second_y", at_y(q)).start()
    left_here(t_recv.at[others_y], "second_y")

    pass_rows(1)
    loads[3].wait()
    loads[4].wait()

    def adam(gradient, columns, target):
        new_first = beta_first * first[:, columns] + (1.0 - beta_first) * gradient
        new_second = beta_second * second[:, columns] + (1.0 - beta_second) * gradient * gradient
        first_hat = new_first / (1.0 - beta_first**STEP)
        second_hat = new_second / (1.0 - beta_second**STEP)
        first_out[:, columns] = new_first
        second_out[:, columns] = new_second
        target[x, y, c] = (first_hat / (jnp.sqrt(second_hat) + adam_eps)).astype(bf16)

    def x_from(o):
        return (x + NX - o) % NX

    def y_from(q):
        return (y + NY - q) % NY

    def x_one(o):
        ref = dir_one.at[x, y, c]
        return move(ref, ref, "x_one", at_x(o), o)

    def y_one(q, o):
        ref = dir_one.at[x_from(o), y, c]
        return move(ref, ref, "y_one", at_y(q), o)

    def y_two(q):
        ref = dir_two.at[x, y, c]
        return move(ref, ref, "y_two", at_y(q), q)

    def x_two(q, o):
        ref = dir_two.at[x, y_from(q), c]
        return move(ref, ref, "x_two", at_x(o), o)

    def share(array, name, o):
        ref = array.at[x_from(o), :, c]
        return move(ref, ref, name, at_core)

    arrived(t_recv.at[others_y], "second_y")
    value = t_send[y]
    for q in range(1, NY):
        value = value + t_recv[q]
    adam(value, slice(0, XF), dir_two)
    for q in SIDES:
        y_two(q).start()
    for o in OFFSETS:
        x_two(0, o).start()
    pass_rows(2)
    arrived(u_recv.at[others], "second_x")
    value = sum_y(0)
    for o in range(1, NX):
        value = value + u_recv[o].astype(f32)
    adam(value, slice(XF, FF), dir_one)
    for o in OFFSETS:
        x_one(o).start()
    for q in SIDES:
        y_one(q, 0).start()
    pass_rows(3)
    for q in SIDES:
        y_two(q).wait_recv()
        for o in OFFSETS:
            x_two(q, o).start()
    share(dir_two, "core_two", 0).start()
    for o in NEAR:
        x_one(o).wait_recv()
        for q in SIDES:
            y_one(q, o).start()
    for o in NEAR:
        arrived(dir_two.at[x_from(o), :, c], "x_two", o)
        share(dir_two, "core_two", o).start()
    for o in (0,) + NEAR:
        arrived(dir_one.at[x_from(o), pl.ds(0, NY - 1), c], "y_one", o)
        share(dir_one, "core_one", o).start()
    left_here(dir_one.at[others, 0, c], "x_one")
    left_here(dir_one.at[:, pl.ds(0, NY - 1), c], "y_one")
    left_here(dir_two.at[0, pl.ds(0, NY - 1), c], "y_two")
    left_here(dir_two.at[others, :, c], "x_two")
    left_here(dir_one.at[:, :, c], "core_one")
    left_here(dir_two.at[:, :, c], "core_two")

    @pl.when(jnp.logical_or(right == NZ // 2, left == NZ // 2 - 1))
    def _():
        rows_z(0).wait_recv()

    arrived(dir_two.at[:, :, 1 - c], "core_two")
    step_out[:, :XF] = galore_scale * jnp.dot(
        rows[...], dir_two[...].reshape(RANK, XF), preferred_element_type=f32
    )
    arrived(dir_one.at[:, :, 1 - c], "core_one")
    step_out[:, XF:] = galore_scale * jnp.dot(
        rows[...], dir_one[...].reshape(RANK, YF), preferred_element_type=f32
    )
    finish()


def body(activations, out_grads, basis, first_moment, second_moment):
    vmem = pl.BlockSpec(memory_space=pltpu.VMEM)
    return pl.pallas_call(
        kernel,
        out_shape=(
            jax.ShapeDtypeStruct((128, FF), f32),
            jax.ShapeDtypeStruct((ROWS, FF), f32),
            jax.ShapeDtypeStruct((ROWS, FF), f32),
        ),
        in_specs=[pl.BlockSpec(memory_space=pl.ANY)] * 5,
        out_specs=(vmem,) * 3,
        scratch_shapes=[
            pltpu.VMEM((TOK, 512), bf16),
            pltpu.VMEM((TOK, FF), bf16),
            pltpu.VMEM((512, RANK), bf16),
            pltpu.VMEM((ROWS, FF), f32),
            pltpu.VMEM((ROWS, FF), f32),
            pltpu.VMEM((CHUNK, TOK), f32),
            pltpu.VMEM((PARTS, NZ, PART, TOK), bf16),
            pltpu.VMEM((PARTS, NZ, PART, TOK), bf16),
            pltpu.VMEM((PARTS, PART, TOK), f32),
            pltpu.VMEM((PARTS, PART, TOK), f32),
            pltpu.VMEM((CHUNK, TOK), bf16),
            pltpu.VMEM((NZ, CHUNK, TOK), bf16),
            pltpu.VMEM((NX, NY, 2, ROWS, FF), f32),
            pltpu.VMEM((NX, NY, ROWS, FF), f32),
            pltpu.VMEM((NX, NY, ROWS, FF), f32),
            pltpu.VMEM((NX, NY, ROWS, XF), bf16),
            pltpu.VMEM((NX, NY, ROWS, XF), bf16),
            pltpu.VMEM((NX, NY, ROWS, YF), bf16),
            pltpu.VMEM((NY, NX, ROWS, YF), bf16),
            pltpu.VMEM((NY, ROWS, XF), f32),
            pltpu.VMEM((NY, ROWS, XF), f32),
            pltpu.VMEM((NX, ROWS, YF), bf16),
            pltpu.VMEM((NX, ROWS, YF), bf16),
            pltpu.VMEM((NX, NY, 2, ROWS, YF), bf16),
            pltpu.VMEM((NX, NY, 2, ROWS, XF), bf16),
            pltpu.VMEM((128, RANK), bf16),
            pltpu.SemaphoreType.DMA((SENDS,)),
            pltpu.SemaphoreType.DMA((RECVS,)),
            pltpu.SemaphoreType.DMA((5,)),
        ],
        compiler_params=pltpu.CompilerParams(
            collective_id=0, has_side_effects=True, vmem_limit_bytes=60 << 20
        ),
        cost_estimate=pl.CostEstimate(flops=10**9, bytes_accessed=4 << 20, transcendentals=0),
        name="galore_step",
    )(activations, out_grads, basis, first_moment, second_moment)


def solution(mesh):
    return jax.shard_map(
        body,
        mesh=mesh,
        in_specs=(P("dp", "mp"), P("dp", "mp"), P("mp", None), P("dp", "mp"), P("dp", "mp")),
        out_specs=(P("dp", "mp"), P("dp", "mp"), P("dp", "mp")),
        check_vma=False,
    )
```

time: 94.7 us -> 91.4 us (0.965)
  Pallas kernels: 90.5 us -> 87.2 us
    pallas_call x1, Pallas kernels: 90.5 us -> 87.2 us  [body(): pl.pallas_call(kernel, out_shape=(jax.ShapeDtypeStruct((128, FF), f32), j...]
where the time goes in v3:
time: 91.4 us; the launch traced here: 91.2 us
  Pallas kernels  87.2 us (95%)
  local copies, waits for them, and re-layouts  3.3 us (4%)
    pallas_call x1, Pallas kernels, body(): pl.pallas_call(kernel, out_shape=(jax.ShapeDtypeStruct((128, FF), f32), j...  87.2 us
    unnamed x7, local copies, waits for them, and re-layouts  3.3 us

profile of v3, /device:TPU:1, one launch (start us, length us, event | category | flops | bytes accessed | tf_op | source)
XLA Modules:
  0.0 91.2 jit_solution(9118866828738750634)
XLA Ops:
  0.6 87.2 %galore_step.1 = (f32[128,896]{1,0:T(8,128)}, f32[16,896]{1,0:T(8,128)}, f32[16,896]{1,0:T(8,128)}) custom-call(bf16[256,512]{1,0:T(8,128)(2,1)} %act_in.1, bf16[256,896]{1,0:T(8,128)(2,1)} %grads_in.1, bf16[512,1024]{1,0:T(8,128)(2,1)} %basis_in.1, f32[16,896]{1,0:T(8,128)} %first_in.1, f32[16,896]{1,0:T(8,128)} %second_in.1), custom_call_target="tpu_custom_call" | custom-call | flops 1000000000 | bytes 4194304 | tf_op jit(solution)/shard_map/galore_step/pallas_call | solution.py:387
  87.9 0.0 copy-start.1
  87.9 1.8 %copy.11 = f32[128,896]{1,0:T(8,128)} copy(f32[128,896]{1,0:T(8,128)} %get-tuple-element.6) | data formatting | bytes 917504
  89.7 0.0 copy-done.1
  89.7 0.0 copy-start
  89.7 0.6 copy.12
  90.3 0.2 copy-done
  90.6 0.6 copy.13
Async XLA Ops:
  87.9 1.8 %copy-start.1 = (f32[16,896]{1,0:T(8,128)S(1)}, f32[16,896]{1,0:T(8,128)}, u32[]{:S(2)}) copy-start(f32[16,896]{1,0:T(8,128)} %get-tuple-element.7) | copy-start | bytes 172036
  89.7 0.8 copy-start

commit v4 on v3

--- a/solution.py
+++ b/solution.py
@@ -19,7 +19,6 @@
 CHUNK = RANK // NX
 PARTS = 2
 PART = CHUNK // PARTS
-PART_Y = NY // PARTS
 BEHIND = 3
 ROWS = 16
 XF = 384
@@ -31,7 +30,7 @@
 f32, bf16 = jnp.float32, jnp.bfloat16
 
 EXCHANGES = {
-    "reduce_z": (1, PARTS), "pair_h": (1, PARTS), "gather_z": (1, PARTS * NZ), "pair_core": (1, PARTS * NX),
+    "reduce_z": (1, PARTS), "pair_h": (1, PARTS), "gather_z": (1, PARTS * NZ), "pair_core": (1, NX),
     "first_x": (1, 1), "first_y": (1, NX), "second_y": (1, 1), "second_x": (1, 1),
     "x_one": (1, NX), "y_one": (1, NX), "y_two": (1, NY), "x_two": (1, NX), "core_one": (1, 1), "core_two": (1, 1),
     "rows_h": (1, 1), "rows_z": (2, 1),
@@ -131,15 +130,16 @@
         return pl.ds(pl.multiple_of((z + k + x) % NX * CHUNK, CHUNK), CHUNK)
 
     def project(k):
-        return jnp.transpose(jnp.dot(act[...], basis[:, columns(k)], preferred_element_type=f32))
+        value = jnp.transpose(jnp.dot(act[...], basis[:, columns(k)], preferred_element_type=f32))
+        value = value.reshape(NY, PARTS, ROWS, TOK)
+        return [value[:, p].reshape(PART, TOK) for p in range(PARTS)]
 
     def reduce_z(p, k):
         return move(part_send.at[p, k], part_recv.at[p, k], "reduce_z", at_z(k), p)
 
     for i, k in enumerate(OFFSETS):
-        value = project(k).astype(bf16)
-        for p in range(PARTS):
-            part_send[p, k] = value[p * PART : (p + 1) * PART]
+        for p, value in enumerate(project(k)):
+            part_send[p, k] = value.astype(bf16)
         if i == 0:
             pl.semaphore_wait(barrier, len(partners))
         reduce_z(0, k).start()
@@ -163,9 +163,10 @@
     def pair_h(p):
         return move(half.at[p], half_recv.at[p], "pair_h", at_h, p)
 
-    own[...] = project(0)
+    for p, value in enumerate(project(0)):
+        own[p] = value
     for p in range(PARTS):
-        total = own[p * PART : (p + 1) * PART, :]
+        total = own[p]
         arrived(part_recv.at[p, others], "reduce_z", p)
         for k in range(1, NZ):
             total = total + part_recv[p, k].astype(f32)
@@ -186,35 +187,30 @@
     def away(k):
         return (z - k + NZ) % NX
 
-    def ys(p):
-        return pl.ds(p * PART_Y, PART_Y)
-
     def to_core(p, k):
-        return move(full.at[k, ys(p), 1 - c], core_recv.at[k, ys(p)], "pair_core", at_core, p * NX + k)
-
-    def to_x(p, o):
-        return move(x_send.at[o, ys(p)], x_recv.at[o, ys(p)], "first_x", at_x(o))
+        return move(full.at[k, p], core_recv.at[k], "pair_core", at_core, k)
+
+    def to_x(o):
+        return move(x_send.at[o], x_recv.at[o], "first_x", at_x(o))
 
     def to_y(q, o):
         return move(y_send.at[o, (y + q) % NY], y_recv.at[q, o], "first_y", at_y(q), o)
 
     def sum_cores(p, k):
-        to_core(p, k).wait_recv()
-        o = away(k)
-        both = full[k, ys(p), c] + core_recv[k, ys(p)]
-        mine[o, ys(p)] = both
-        x_send[o, ys(p)] = both[:, :, :XF].astype(bf16)
-        y_send[o, ys(p)] = both[:, :, XF:].astype(bf16)
-
-        @pl.when(o != 0)
+        @pl.when(c == p)
         def _():
-            to_x(p, o).start()
-
-        for i in range(PART_Y):
-            q = (p * PART_Y + i - y + NY) % NY
-
-            @pl.when(q != 0)
+            to_core(p, k).wait_recv()
+            o = away(k)
+            both = full[k, p] + core_recv[k]
+            mine[o] = both
+            x_send[o] = both[:, :, :XF].astype(bf16)
+            y_send[o] = both[:, :, XF:].astype(bf16)
+
+            @pl.when(o != 0)
             def _():
+                to_x(o).start()
+
+            for q in SIDES:
                 to_y(q, o).start()
 
     def gradient(p, k):
@@ -224,8 +220,11 @@
         else:
             block = turned[pl.ds(p * PART, PART), :]
         product = jnp.dot(block, grads[...], preferred_element_type=f32)
-        full[k, ys(p)] = product.reshape(PART_Y, 2, ROWS, FF)
-        to_core(p, k).start()
+        full[k, p] = product.reshape(NY, ROWS, FF)
+
+        @pl.when(c != p)
+        def _():
+            to_core(p, k).start()
 
     loads[2].wait()
     work = [(p, k) for p in range(PARTS) for k in (0,) + NEAR]
@@ -399,14 +398,14 @@
             pltpu.VMEM((512, RANK), bf16),
             pltpu.VMEM((ROWS, FF), f32),
             pltpu.VMEM((ROWS, FF), f32),
-            pltpu.VMEM((CHUNK, TOK), f32),
+            pltpu.VMEM((PARTS, PART, TOK), f32),
             pltpu.VMEM((PARTS, NZ, PART, TOK), bf16),
             pltpu.VMEM((PARTS, NZ, PART, TOK), bf16),
             pltpu.VMEM((PARTS, PART, TOK), f32),
             pltpu.VMEM((PARTS, PART, TOK), f32),
             pltpu.VMEM((CHUNK, TOK), bf16),
             pltpu.VMEM((NZ, CHUNK, TOK), bf16),
-            pltpu.VMEM((NX, NY, 2, ROWS, FF), f32),
+            pltpu.VMEM((NX, PARTS, NY, ROWS, FF), f32),
             pltpu.VMEM((NX, NY, ROWS, FF), f32),
             pltpu.VMEM((NX, NY, ROWS, FF), f32),
             pltpu.VMEM((NX, NY, ROWS, XF), bf16),

time: 91.4 us -> 90.7 us (level)
  no operation moved by 1% of the time
where the time goes in v4:
time: 90.7 us; the launch traced here: 90.4 us
  Pallas kernels  86.5 us (95%)
  local copies, waits for them, and re-layouts  3.3 us (4%)
    pallas_call x1, Pallas kernels, body(): pl.pallas_call(kernel, out_shape=(jax.ShapeDtypeStruct((128, FF), f32), j...  86.5 us
    unnamed x7, local copies, waits for them, and re-layouts  3.3 us

profile of v4, /device:TPU:1, one launch (start us, length us, event | category | flops | bytes accessed | tf_op | source)
XLA Modules:
  0.0 90.4 jit_solution(15481101403067881276)
XLA Ops:
  0.6 86.5 %galore_step.1 = (f32[128,896]{1,0:T(8,128)}, f32[16,896]{1,0:T(8,128)}, f32[16,896]{1,0:T(8,128)}) custom-call(bf16[256,512]{1,0:T(8,128)(2,1)} %act_in.1, bf16[256,896]{1,0:T(8,128)(2,1)} %grads_in.1, bf16[512,1024]{1,0:T(8,128)(2,1)} %basis_in.1, f32[16,896]{1,0:T(8,128)} %first_in.1, f32[16,896]{1,0:T(8,128)} %second_in.1), custom_call_target="tpu_custom_call" | custom-call | flops 1000000000 | bytes 4194304 | tf_op jit(solution)/shard_map/galore_step/pallas_call | solution.py:386
  87.1 0.0 copy-start.1
  87.1 1.8 %copy.11 = f32[128,896]{1,0:T(8,128)} copy(f32[128,896]{1,0:T(8,128)} %get-tuple-element.6) | data formatting | bytes 917504
  89.0 0.0 copy-done.1
  89.0 0.0 copy-start
  89.0 0.6 copy.12
  89.6 0.2 copy-done
  89.8 0.6 copy.13
Async XLA Ops:
  87.1 1.8 %copy-start.1 = (f32[16,896]{1,0:T(8,128)S(1)}, f32[16,896]{1,0:T(8,128)}, u32[]{:S(2)}) copy-start(f32[16,896]{1,0:T(8,128)} %get-tuple-element.7) | copy-start | bytes 172036
  89.0 0.8 copy-start

commit v5 on v4

--- a/solution.py
+++ b/solution.py
@@ -26,6 +26,8 @@
 OFFSETS = (4, 3, 5, 2, 6, 1, 7)
 NEAR = (1, 7, 2, 6, 3, 5, 4)
 SIDES = (1, 3, 2)
+RELAY = (3, 5)
+GATHER = ((1, 7, 3, 2, 6, 5, 4), (1, 7, 5, 2, 6, 3, 4))
 
 f32, bf16 = jnp.float32, jnp.bfloat16
 
@@ -103,10 +105,6 @@
 
     loads[0].wait()
     loads[1].wait()
-
-    @pl.when(owns)
-    def _():
-        rows[...] = basis[pl.ds(pl.multiple_of((y % 2 * 2 + c) * 128, 128), 128), :]
 
     def rows_h():
         return move(rows, rows, "rows_h", at_h)
@@ -152,6 +150,7 @@
 
     @pl.when(owns)
     def _():
+        rows[...] = basis[pl.ds(pl.multiple_of((y % 2 * 2 + c) * 128, 128), 128), :]
         rows_h().start()
 
     def sent_rows_h():
@@ -178,11 +177,19 @@
         ranks = pl.ds(p * PART, PART)
         return move(turned.at[ranks], turned_recv.at[k, ranks], "gather_z", at_z(k), p * NZ + k)
 
+    def relay_z(p):
+        ranks = pl.ds(p * PART, PART)
+        device = at_z(1 if RELAY[p] < NZ // 2 else NZ - 1)
+        place = p * NZ + NZ // 2
+        return move(turned_recv.at[RELAY[p], ranks], turned_recv.at[NZ // 2, ranks], "gather_z", device, place)
+
     def gather(p):
         pair_h(p).wait_recv()
         turned[pl.ds(p * PART, PART), :] = (half[p] + half_recv[p]).astype(bf16)
-        for k in NEAR:
-            gather_z(p, k).start()
+        gather_z(p, RELAY[p]).start()
+        for k in GATHER[p]:
+            if k not in (RELAY[p], NZ // 2):
+                gather_z(p, k).start()
 
     def away(k):
         return (z - k + NZ) % NX
@@ -216,6 +223,8 @@
     def gradient(p, k):
         if k:
             gather_z(p, k).wait_recv()
+            if k == RELAY[p]:
+                relay_z(p).start()
             block = turned_recv[k, pl.ds(p * PART, PART)]
         else:
             block = turned[pl.ds(p * PART, PART), :]
@@ -227,7 +236,7 @@
             to_core(p, k).start()
 
     loads[2].wait()
-    work = [(p, k) for p in range(PARTS) for k in (0,) + NEAR]
+    work = [(p, k) for p in range(PARTS) for k in (0,) + GATHER[p]]
     gather(0)
     for i, (p, k) in enumerate(work):
         gradient(p, k)

time: 90.7 us -> 92.5 us (1.020)
  the two profiles are of different devices: /device:TPU:1 before, /device:TPU:11 now
where the time goes in v5:
time: 92.5 us; the launch traced here: 92.2 us
  Pallas kernels  88.3 us (95%)
  local copies, waits for them, and re-layouts  3.3 us (4%)
    pallas_call x1, Pallas kernels, body(): pl.pallas_call(kernel, out_shape=(jax.ShapeDtypeStruct((128, FF), f32), j...  88.3 us
    unnamed x7, local copies, waits for them, and re-layouts  3.3 us

profile of v5, /device:TPU:11, one launch (start us, length us, event | category | flops | bytes accessed | tf_op | source)
XLA Modules:
  0.0 92.2 jit_solution(10968301136933331411)
XLA Ops:
  0.6 88.3 %galore_step.1 = (f32[128,896]{1,0:T(8,128)}, f32[16,896]{1,0:T(8,128)}, f32[16,896]{1,0:T(8,128)}) custom-call(bf16[256,512]{1,0:T(8,128)(2,1)} %act_in.1, bf16[256,896]{1,0:T(8,128)(2,1)} %grads_in.1, bf16[512,1024]{1,0:T(8,128)(2,1)} %basis_in.1, f32[16,896]{1,0:T(8,128)} %first_in.1, f32[16,896]{1,0:T(8,128)} %second_in.1), custom_call_target="tpu_custom_call" | custom-call | flops 1000000000 | bytes 4194304 | tf_op jit(solution)/shard_map/galore_step/pallas_call | solution.py:395
  88.9 0.0 copy-start.1
  88.9 1.8 %copy.11 = f32[128,896]{1,0:T(8,128)} copy(f32[128,896]{1,0:T(8,128)} %get-tuple-element.6) | data formatting | bytes 917504
  90.8 0.0 copy-done.1
  90.8 0.0 copy-start
  90.8 0.6 copy.12
  91.4 0.2 copy-done
  91.6 0.6 copy.13
Async XLA Ops:
  88.9 1.8 %copy-start.1 = (f32[16,896]{1,0:T(8,128)S(1)}, f32[16,896]{1,0:T(8,128)}, u32[]{:S(2)}) copy-start(f32[16,896]{1,0:T(8,128)} %get-tuple-element.7) | copy-start | bytes 172036
  90.8 0.8 copy-start

commit v6 on v4

--- a/solution.py
+++ b/solution.py
@@ -170,7 +170,8 @@
         arrived(part_recv.at[p, others], "reduce_z", p)
         for k in range(1, NZ):
             total = total + part_recv[p, k].astype(f32)
-        half[p] = total
+        own[p] = total
+        half[p] = total.astype(bf16)
         pair_h(p).start()
     left_here(half, "pair_h")
 
@@ -180,7 +181,7 @@
 
     def gather(p):
         pair_h(p).wait_recv()
-        turned[pl.ds(p * PART, PART), :] = (half[p] + half_recv[p]).astype(bf16)
+        turned[pl.ds(p * PART, PART), :] = (own[p] + half_recv[p].astype(f32)).astype(bf16)
         for k in NEAR:
             gather_z(p, k).start()
 
@@ -401,8 +402,8 @@
             pltpu.VMEM((PARTS, PART, TOK), f32),
             pltpu.VMEM((PARTS, NZ, PART, TOK), bf16),
             pltpu.VMEM((PARTS, NZ, PART, TOK), bf16),
-            pltpu.VMEM((PARTS, PART, TOK), f32),
-            pltpu.VMEM((PARTS, PART, TOK), f32),
+            pltpu.VMEM((PARTS, PART, TOK), bf16),
+            pltpu.VMEM((PARTS, PART, TOK), bf16),
             pltpu.VMEM((CHUNK, TOK), bf16),
             pltpu.VMEM((NZ, CHUNK, TOK), bf16),
             pltpu.VMEM((NX, PARTS, NY, ROWS, FF), f32),

time: 90.7 us -> 89.5 us (0.987)
  the two profiles are of different devices: /device:TPU:1 before, /device:TPU:11 now
where the time goes in v6:
time: 89.5 us; the launch traced here: 89.3 us
  Pallas kernels  85.3 us (95%)
  local copies, waits for them, and re-layouts  3.3 us (4%)
    pallas_call x1, Pallas kernels, body(): pl.pallas_call(kernel, out_shape=(jax.ShapeDtypeStruct((128, FF), f32), j...  85.3 us
    unnamed x7, local copies, waits for them, and re-layouts  3.3 us

profile of v6, /device:TPU:11, one launch (start us, length us, event | category | flops | bytes accessed | tf_op | source)
XLA Modules:
  0.0 89.3 jit_solution(2082354730560465321)
XLA Ops:
  0.6 85.3 %galore_step.1 = (f32[128,896]{1,0:T(8,128)}, f32[16,896]{1,0:T(8,128)}, f32[16,896]{1,0:T(8,128)}) custom-call(bf16[256,512]{1,0:T(8,128)(2,1)} %act_in.1, bf16[256,896]{1,0:T(8,128)(2,1)} %grads_in.1, bf16[512,1024]{1,0:T(8,128)(2,1)} %basis_in.1, f32[16,896]{1,0:T(8,128)} %first_in.1, f32[16,896]{1,0:T(8,128)} %second_in.1), custom_call_target="tpu_custom_call" | custom-call | flops 1000000000 | bytes 4194304 | tf_op jit(solution)/shard_map/galore_step/pallas_call | solution.py:387
  86.0 0.0 copy-start.1
  86.0 1.8 %copy.11 = f32[128,896]{1,0:T(8,128)} copy(f32[128,896]{1,0:T(8,128)} %get-tuple-element.6) | data formatting | bytes 917504
  87.8 0.0 copy-done.1
  87.8 0.0 copy-start
  87.8 0.6 copy.12
  88.4 0.2 copy-done
  88.7 0.6 copy.13
Async XLA Ops:
  86.0 1.8 %copy-start.1 = (f32[16,896]{1,0:T(8,128)S(1)}, f32[16,896]{1,0:T(8,128)}, u32[]{:S(2)}) copy-start(f32[16,896]{1,0:T(8,128)} %get-tuple-element.7) | copy-start | bytes 172036
  87.8 0.8 copy-start
